TPU v7x, 512 devices: a whole 4x8x8 slice. The times are simulated.
512 devices in a mesh: rows: 64 (over x, y, core), probe: 8 (over z).
Axes of the slice: x: 4, y: 8, z: 8, core: 2. Of those that a mesh axis runs over, the one named last changes fastest.
Arguments:
- targets: float32 [3, 65536], P(None, 'rows'), may hold values from 0 to 1
- sources: bfloat16 [3, 8192], P(None, 'rows'), may hold values from 0 to 1
- probes: bfloat16 [256, 8192], P('probe', 'rows'), may hold values from -6 to 6
- cluster_sizes: int32 [512], P(('rows', 'probe')), may hold values from 64 to 128, as said below
- leaf_ranks: int32 [512], P(('rows', 'probe')), may hold values from 128 to 256, as said below
Outputs:
- leaf_basis: float32 [256, 2, 65536], P(None, None, ('rows', 'probe'))
- top_factor: float32 [512, 256, 256], P(('rows', 'probe'))
Inputs may be any that keep to these rules, and one draw needn't show every extreme that they name: `cluster_sizes`: some leaf uses all 128 points in every draw. `leaf_ranks`: some leaf keeps all 256 rows in every draw.
All inputs are finite; a program needn't handle non-finite values.
Results may differ from a plain program's by a relative error of at most 0.0033.
Values may be sent and summed in bfloat16 or wider, within the bound.
A program may use at most 64 MiB of HBM per device.

v0:
```python
import math
import jax
import jax.numpy as jnp
from jax import lax
from jax.sharding import PartitionSpec as P

wavenumber = 30.0
softening = 0.02


def partner_2(value, axis, apart):
    mask = 2**apart
    pairs = [(source, source ^ mask) for source in range(lax.axis_size(axis))]
    return lax.ppermute(value, axis, pairs)


def kernel_pair(source_pts, target_pts, col_total):
    diff_x = source_pts[0][:, None] - target_pts[0][None, :]
    diff_y = source_pts[1][:, None] - target_pts[1][None, :]
    diff_z = source_pts[2][:, None] - target_pts[2][None, :]
    distance = jnp.sqrt(diff_x * diff_x + diff_y * diff_y + diff_z * diff_z + softening * softening)
    amplitude = 1.0 / (distance * jnp.sqrt(jnp.float32(col_total)))
    kernel_cos = (amplitude * jnp.cos(wavenumber * distance)).astype(jnp.bfloat16)
    kernel_sin = (amplitude * jnp.sin(wavenumber * distance)).astype(jnp.bfloat16)
    return (kernel_cos, kernel_sin)


def sample_block(probe_piece, source_piece, target_pts, col_total):
    columns = probe_piece.shape[1]
    block_cols = math.gcd(columns, 256)
    block_count = columns // block_cols
    probe_parts = probe_piece.reshape(probe_piece.shape[0], block_count, block_cols).transpose(
        1, 0, 2
    )
    source_parts = source_piece.reshape(3, block_count, block_cols).transpose(1, 0, 2)

    def advance(running, pieces):
        probe_part, source_part = pieces
        kernel_cos, kernel_sin = kernel_pair(source_part.astype(jnp.float32), target_pts, col_total)
        part_cos = jnp.dot(probe_part, kernel_cos, preferred_element_type=jnp.float32)
        part_sin = jnp.dot(probe_part, kernel_sin, preferred_element_type=jnp.float32)
        return (running + jnp.stack([part_cos, part_sin]), None)

    starting = jnp.zeros((2, probe_piece.shape[0], target_pts.shape[1]), jnp.float32)
    result, _ = lax.scan(advance, starting, (probe_parts, source_parts))
    return result


def make_adder(target_pts, col_total):

    def add_columns(running, pieces, offset_col):
        return sample_block(pieces[0], pieces[1], target_pts, col_total)

    return add_columns


def cholesky_basis(matrix, nprobe_total):
    gram_matrix = jnp.dot(matrix, matrix.T, precision=lax.Precision.HIGHEST)
    shift_value = jnp.trace(gram_matrix) / nprobe_total
    factor = jnp.linalg.cholesky(
        gram_matrix + shift_value * jnp.eye(nprobe_total, dtype=matrix.dtype)
    )
    return jax.scipy.linalg.solve_triangular(factor, matrix, lower=True)


def per_device(targets, sources, probes, cluster_sizes, leaf_ranks):
    col_total = sources.shape[1] * lax.axis_size("rows")
    nprobe_total = probes.shape[0] * lax.axis_size("probe")
    leaf_rows = targets.shape[1] // lax.axis_size("probe")
    own_targets = lax.dynamic_slice_in_dim(
        targets, lax.axis_index("probe") * leaf_rows, leaf_rows, 1
    )
    all_probes = lax.all_gather(probes, "probe", axis=0, tiled=True)
    adder = make_adder(own_targets, col_total)
    starting = jnp.zeros((2, nprobe_total, leaf_rows), jnp.float32)
    samples = adder(
        starting,
        (
            lax.all_gather(all_probes, "rows", axis=1, tiled=True),
            lax.all_gather(sources, "rows", axis=1, tiled=True),
        ),
        jnp.int32(0),
    )
    kept_rows = (jnp.arange(leaf_rows) < cluster_sizes[0]).astype(jnp.float32)
    matrix = jnp.concatenate([samples[0] * kept_rows, samples[1] * kept_rows], axis=1)
    basis_rows = cholesky_basis(matrix, nprobe_total)
    rank_rows = (jnp.arange(nprobe_total) < leaf_ranks[0]).astype(jnp.float32)
    basis_rows = basis_rows * rank_rows[:, None]
    projected = jnp.dot(matrix, basis_rows.T, precision=lax.Precision.HIGHEST)
    row_index = lax.axis_index("rows")
    for tree_bit in range(2):
        partner = partner_2(projected, "rows", tree_bit)
        is_left = row_index >> tree_bit & 1 == 0
        left_part = jnp.where(is_left, projected, partner)
        right_part = jnp.where(is_left, partner, projected)
        stacked = jnp.concatenate([left_part, right_part], axis=1)
        node_basis = cholesky_basis(stacked, nprobe_total)
        projected = jnp.dot(stacked, node_basis.T, precision=lax.Precision.HIGHEST)
    return (basis_rows.reshape(nprobe_total, 2, leaf_rows), projected[None])


def solution(mesh):
    return jax.shard_map(
        per_device,
        mesh=mesh,
        in_specs=(
            P(None, "rows"),
            P(None, "rows"),
            P("probe", "rows"),
            P(("rows", "probe")),
            P(("rows", "probe")),
        ),
        out_specs=(P(None, None, ("rows", "probe")), P(("rows", "probe"), None, None)),
        check_vma=False,
    )
```

profile of v0, /device:TPU:1, one launch (start us, length us, event | category | flops | bytes accessed | tf_op | source)
XLA Modules:
  0.0 452.6 jit_solution(17370533172197070458)
XLA Ops:
  7.2 25.9 %all_gather.9 = bf16[256,128]{1,0:T(8,128)(2,1)S(1)} all-gather(bf16[32,128]{1,0:T(8,128)(2,1)} %param.12), channel_id=1, replica_groups=mesh['rows'=64,'probe'=8] {'probe'}, dimensions={0}, use_global_device_ids=true | all-gather | bytes 73728 | tf_op jit(solution)/shard_map/all_gather | solution.py:73
  35.2 46.2 %all_gather.11 = bf16[3,8192]{1,0:T(4,128)(2,1)S(1)} all-gather(bf16[3,128]{1,0:T(4,128)(2,1)} %param.11), channel_id=1, replica_groups=mesh['rows'=64,'probe'=8] {'rows'}, dimensions={1}, use_global_device_ids=true | all-gather | bytes 49920 | tf_op jit(solution)/shard_map/all_gather | solution.py:80
  81.4 41.8 %all-gather.2.cloned.1.call-done = bf16[256,8192]{0,1:T(8,128)(2,1)} async-done(((bf16[256,128]{0,1:T(8,128)(2,1)}), bf16[256,8192]{0,1:T(8,128)(2,1)}) %all-gather.2.cloned.1.call-update) | async-done | bytes 4194320 | tf_op jit(solution)/shard_map/all_gather | solution.py:79
  123.2 113.8 %while.17 = (s32[]{:T(128)}, f32[2,256,128]{2,1,0:T(8,128)S(1)}, bf16[32,256,256]{1,2,0:T(8,128)(2,1)}, bf16[32,3,256]{2,1,0:T(4,128)(2,1)S(1)}, f32[3,128]{1,0:T(4,128)S(1)}, /*index=5*/s32[]{:T(128)}, s32[]{:T(128)}) while((s32[]{:T(128)}, f32[2,256,128]{2,1,0:T(8,128)S(1)}, bf16[32,256,256]{1,2,0:T(8,128)(2,1)}, ...), condition=%wide.region_1.2_spmd.clone, body=%wide.region_0.1_spmd.clone.sunk | while | flops 34669312 | bytes 1334875 | solution.py:45
  132.0 1.7 convolution_bitcast_fusion.5
  142.6 1.7 convolution_bitcast_fusion.5
  153.3 1.7 convolution_bitcast_fusion.5
  163.9 1.7 convolution_bitcast_fusion.5
  174.5 1.7 convolution_bitcast_fusion.5
  185.1 1.7 convolution_bitcast_fusion.5
  195.8 1.7 convolution_bitcast_fusion.5
  206.4 1.7 convolution_bitcast_fusion.5
  217.0 1.7 convolution_bitcast_fusion.5
  239.0 11.7 %cholesky.172 = f32[128,128]{1,0:T(8,128)S(1)} custom-call(f32[128,128]{1,0:T(8,128)S(1)} %cholesky.270), custom_call_target="Cholesky" | custom-call | tf_op jit(solution)/shard_map/jit(cholesky)/cholesky | solution.py:60
  250.7 9.8 %custom-call.20 = f32[1,128,128]{1,2,0:T(8,128)S(1)} custom-call(f32[1,128,128]{2,1,0:T(8,128)S(1)} %get-tuple-element.157), custom_call_target="InvertDiagBlocksLowerTriangular" | custom-call | tf_op jit(solution)/shard_map/jit(cholesky)/cholesky | solution.py:60
  261.0 11.7 %cholesky.189 = f32[128,128]{1,0:T(8,128)S(1)} custom-call(f32[128,128]{1,0:T(8,128)S(1)} %convolution_subtract_fusion.3), custom_call_target="Cholesky" | custom-call | tf_op jit(solution)/shard_map/jit(cholesky)/cholesky | solution.py:60
  275.2 4.2 while.16
  279.5 19.8 %custom-call.15 = f32[2,128,128]{1,2,0:T(8,128)S(1)} custom-call(f32[2,128,128]{2,1,0:T(8,128)S(1)} %get-tuple-element.47), custom_call_target="InvertDiagBlocksLowerTriangular" | custom-call | tf_op jit(solution)/shard_map/jit(_solve_triangular)/triangular_solve | solution.py:63
  300.7 2.2 collective-permute-start
  306.7 11.7 %cholesky.206 = f32[128,128]{1,0:T(8,128)S(1)} custom-call(f32[128,128]{1,0:T(8,128)S(1)} %cholesky.273), custom_call_target="Cholesky" | custom-call | tf_op jit(solution)/shard_map/jit(cholesky)/cholesky | solution.py:60
  318.4 9.8 %custom-call.21 = f32[1,128,128]{1,2,0:T(8,128)S(1)} custom-call(f32[1,128,128]{2,1,0:T(8,128)S(1)} %get-tuple-element.155), custom_call_target="InvertDiagBlocksLowerTriangular" | custom-call | tf_op jit(solution)/shard_map/jit(cholesky)/cholesky | solution.py:60
  328.7 11.7 %cholesky.223 = f32[128,128]{1,0:T(8,128)S(1)} custom-call(f32[128,128]{1,0:T(8,128)S(1)} %convolution_subtract_fusion.2), custom_call_target="Cholesky" | custom-call | tf_op jit(solution)/shard_map/jit(cholesky)/cholesky | solution.py:60
  343.2 4.3 while.18
  347.6 19.7 %custom-call.22 = f32[2,128,128]{1,2,0:T(8,128)S(1)} custom-call(f32[2,128,128]{2,1,0:T(8,128)S(1)} %get-tuple-element.72), custom_call_target="InvertDiagBlocksLowerTriangular" | custom-call | tf_op jit(solution)/shard_map/jit(_solve_triangular)/triangular_solve | solution.py:63
  369.4 2.0 collective-permute-start.1
  372.6 6.3 %collective-permute-done.1 = f32[256,256]{0,1:T(8,128)S(1)} collective-permute-done((f32[256,256]{0,1:T(8,128)S(1)}, f32[256,256]{0,1:T(8,128)S(1)}, u32[]{:S(2)}, u32[]{:S(2)}) %collective-permute-start.1) | collective-permute-done | bytes 262176 | tf_op jit(solution)/shard_map/ppermute | solution.py:14
  381.5 11.7 %cholesky.240 = f32[128,128]{1,0:T(8,128)S(1)} custom-call(f32[128,128]{1,0:T(8,128)S(1)} %cholesky.276), custom_call_target="Cholesky" | custom-call | tf_op jit(solution)/shard_map/jit(cholesky)/cholesky | solution.py:60
  393.2 9.8 %custom-call.23 = f32[1,128,128]{1,2,0:T(8,128)S(1)} custom-call(f32[1,128,128]{2,1,0:T(8,128)S(1)} %get-tuple-element.151), custom_call_target="InvertDiagBlocksLowerTriangular" | custom-call | tf_op jit(solution)/shard_map/jit(cholesky)/cholesky | solution.py:60
  403.5 11.7 %cholesky.257 = f32[128,128]{1,0:T(8,128)S(1)} custom-call(f32[128,128]{1,0:T(8,128)S(1)} %convolution_subtract_fusion.1), custom_call_target="Cholesky" | custom-call | tf_op jit(solution)/shard_map/jit(cholesky)/cholesky | solution.py:60
  418.0 4.4 while.19
  422.4 19.7 %custom-call.24 = f32[2,128,128]{1,2,0:T(8,128)S(1)} custom-call(f32[2,128,128]{2,1,0:T(8,128)S(1)} %get-tuple-element.73), custom_call_target="InvertDiagBlocksLowerTriangular" | custom-call | tf_op jit(solution)/shard_map/jit(_solve_triangular)/triangular_solve | solution.py:63
  443.6 1.7 convolution_bitcast_fusion.2
  (280 shorter events, 126.9 us)
Async XLA Ops:
  7.2 74.2 %copy-start = (f32[3,1024]{1,0:T(4,128)S(1)}, f32[3,1024]{1,0:T(4,128)}, u32[]{:S(2)}) copy-start(f32[3,1024]{1,0:T(4,128)} %param.10) | copy-start | bytes 36868
  7.2 116.0 %all-gather.2.cloned.1.call-start = ((), (), s32[]{:S(2)}) async-start(), calls=%async_computation | async-start | bytes 4259840 | tf_op jit(solution)/shard_map/all_gather | solution.py:79
  300.7 3.4 collective-permute-start
  369.4 9.6 %collective-permute-start.1 = (f32[256,256]{0,1:T(8,128)S(1)}, f32[256,256]{0,1:T(8,128)S(1)}, u32[]{:S(2)}, u32[]{:S(2)}) collective-permute-start(f32[256,256]{0,1:T(8,128)S(1)} %fusion.30), channel_id=1, source_target_pairs={{0,16},{8,24},{16,0},{24,8},{32,48},{40,56},{48,32},{56,40},{64,80... | collective-permute-start | bytes 786440 | tf_op jit(solution)/shard_map/ppermute | solution.py:14
Sparse Core Ops, SparseCore 0:
  34.0 89.1 all-gather.1
where the time goes:
time: 457 us; the launch traced here: 453 us
  other arithmetic  167 us (37%)
  matrix products  121 us (26%)
  blocking collectives  72.1 us (16%)
  waiting for transfers between devices  49.3 us (11%)
  between operations  22.2 us (5%)
  local copies, waits for them, and re-layouts  14.3 us (3%)
    another operation x20, other arithmetic, cholesky_basis(): jnp.linalg.cholesky(gram_matrix + shift_value * jnp.eye(nprobe_total, dty...  103 us
    another operation x7, other arithmetic, cholesky_basis(): return jax.scipy.linalg.solve_triangular(factor, matrix, lower=True)  59.3 us
    dot_general x32, matrix products, advance(): jnp.dot(probe_part, kernel_sin, preferred_element_type=jnp.float32)  54.3 us
    dot_general x32, matrix products, advance(): jnp.dot(probe_part, kernel_cos, preferred_element_type=jnp.float32)  54.1 us
    all_gather x1, blocking collectives, per_device(): lax.all_gather(sources, 'rows', axis=1, tiled=True)  46.2 us
    all_gather x1, waiting for transfers between devices, per_device(): lax.all_gather(all_probes, 'rows', axis=1, tiled=True)  41.8 us
    all_gather x1, blocking collectives, per_device(): all_probes = lax.all_gather(probes, 'probe', axis=0, tiled=True)  25.9 us
  transfers between devices with their start and end apart: 3, of which 3 were waited for; matrix products, arithmetic and copies ran while one was open for 0% of the time, Pallas kernels for 0%

commit v1 on v0

--- a/solution.py
+++ b/solution.py
@@ -6,6 +6,15 @@
 
 wavenumber = 30.0
 softening = 0.02
+search_cells_up = lambda base_x, row_axis: jnp.concatenate(
+    jax.lax.all_to_all(
+        jnp.stack([base_x for _ in range(jax.lax.psum(1, row_axis))], 0),
+        row_axis,
+        concat_axis=0,
+        split_axis=0,
+    ),
+    1,
+)
 
 
 def partner_2(value, axis, apart):
@@ -75,10 +84,7 @@
     starting = jnp.zeros((2, nprobe_total, leaf_rows), jnp.float32)
     samples = adder(
         starting,
-        (
-            lax.all_gather(all_probes, "rows", axis=1, tiled=True),
-            lax.all_gather(sources, "rows", axis=1, tiled=True),
-        ),
+        (search_cells_up(all_probes, "rows"), lax.all_gather(sources, "rows", axis=1, tiled=True)),
         jnp.int32(0),
     )
     kept_rows = (jnp.arange(leaf_rows) < cluster_sizes[0]).astype(jnp.float32)

time: 457 us -> 499 us (1.092)
  blocking collectives: 72.1 us -> 150 us
  waiting for transfers between devices: 49.3 us -> 7.75 us
  starting transfers between devices: 4.24 us -> 21.3 us
  between operations: 22.2 us -> 8.8 us
    all_gather x1, blocking collectives: 46.2 us -> 124 us  [per_device(): lax.all_gather(sources, 'rows', axis=1, tiled=True)]
    all_gather x1 -> x0, waiting for transfers between devices: 41.8 us -> none  [per_device(): lax.all_gather(all_probes, 'rows', axis=1, tiled=True)]
    all_to_all x0 -> x1, starting transfers between devices: none -> 17.1 us  [jax.lax.all_to_all(jnp.stack([base_x for _ in range(jax.lax.psum(1, row_a...]
  transfers between devices with their start and end apart: 3 -> 3, of which waited for: 3 -> 2; matrix products, arithmetic and copies ran while one was open for 0% -> 0% of each run, Pallas kernels for 0% -> 0%
where the time goes in v1:
time: 499 us; the launch traced here: 494 us
  other arithmetic  167 us (33%)
  blocking collectives  150 us (30%)
  matrix products  121 us (24%)
  starting transfers between devices  21.3 us (4%)
  local copies, waits for them, and re-layouts  16.2 us (3%)
  between operations  8.8 us (2%)
  waiting for transfers between devices  7.75 us (2%)
    all_gather x1, blocking collectives, per_device(): lax.all_gather(sources, 'rows', axis=1, tiled=True)  124 us
    another operation x20, other arithmetic, cholesky_basis(): jnp.linalg.cholesky(gram_matrix + shift_value * jnp.eye(nprobe_total, dty...  103 us
    another operation x7, other arithmetic, cholesky_basis(): return jax.scipy.linalg.solve_triangular(factor, matrix, lower=True)  59.3 us
    dot_general x32, matrix products, advance(): jnp.dot(probe_part, kernel_sin, preferred_element_type=jnp.float32)  54.2 us
    dot_general x32, matrix products, advance(): jnp.dot(probe_part, kernel_cos, preferred_element_type=jnp.float32)  54 us
    all_gather x1, blocking collectives, per_device(): all_probes = lax.all_gather(probes, 'probe', axis=0, tiled=True)  25.9 us
    all_to_all x1, starting transfers between devices, jax.lax.all_to_all(jnp.stack([base_x for _ in range(jax.lax.psum(1, row_a...  17.1 us
  transfers between devices with their start and end apart: 3, of which 2 were waited for; matrix products, arithmetic and copies ran while one was open for 0% of the time, Pallas kernels for 0%

profile of v1, /device:TPU:1, one launch (start us, length us, event | category | flops | bytes accessed | tf_op | source)
XLA Modules:
  0.0 494.1 jit_solution(17941880421391601033)
XLA Ops:
  0.6 25.9 %all_gather.6 = bf16[256,128]{1,0:T(8,128)(2,1)S(1)} all-gather(bf16[32,128]{1,0:T(8,128)(2,1)} %param.12), channel_id=1, replica_groups=mesh['rows'=64,'probe'=8] {'probe'}, dimensions={0}, use_global_device_ids=true | all-gather | bytes 73728 | tf_op jit(solution)/shard_map/all_gather | solution.py:82
  26.7 2.5 stack.8
  29.2 17.1 %all-to-all-start = ((bf16[64,256,128]{1,2,0:T(8,128)(2,1)}), bf16[64,256,128]{1,2,0:T(8,128)(2,1)}, u32[]{:S(2)}, u32[]{:S(2)}) async-start(bf16[64,256,128]{1,2,0:T(8,128)(2,1)} %stack.8), calls=%async_computation | async-start | bytes 8388608 | tf_op jit(solution)/shard_map/all_to_all | solution.py:10
  47.6 123.7 %all_gather.7 = bf16[3,8192]{1,0:T(4,128)(2,1)S(1)} all-gather(bf16[3,128]{1,0:T(4,128)(2,1)S(1)} %copy-done.1), channel_id=1, replica_groups=mesh['rows'=64,'probe'=8] {'rows'}, dimensions={1}, use_global_device_ids=true | all-gather | bytes 49920 | tf_op jit(solution)/shard_map/all_gather | solution.py:87
  171.4 113.8 %while.17 = (s32[]{:T(128)}, f32[2,256,128]{2,1,0:T(8,128)S(1)}, bf16[32,256,256]{1,2,0:T(8,128)(2,1)}, bf16[32,3,256]{2,1,0:T(4,128)(2,1)S(1)}, f32[3,128]{1,0:T(4,128)S(1)}, /*index=5*/s32[]{:T(128)}, s32[]{:T(128)}) while((s32[]{:T(128)}, f32[2,256,128]{2,1,0:T(8,128)S(1)}, bf16[32,256,256]{1,2,0:T(8,128)(2,1)}, ...), condition=%wide.region_1.2_spmd.clone, body=%wide.region_0.1_spmd.clone.sunk | while | flops 34669312 | bytes 1334875 | solution.py:54
  180.2 1.7 convolution_bitcast_fusion.5
  187.3 1.7 convolution_bitcast_fusion.5
  194.4 1.7 convolution_bitcast_fusion.5
  201.4 1.7 convolution_bitcast_fusion.5
  208.5 1.7 convolution_bitcast_fusion.5
  215.6 1.7 convolution_bitcast_fusion.5
  222.7 1.7 convolution_bitcast_fusion.5
  258.1 1.7 convolution_bitcast_fusion.5
  287.1 11.7 %cholesky.172 = f32[128,128]{1,0:T(8,128)S(1)} custom-call(f32[128,128]{1,0:T(8,128)S(1)} %cholesky.270), custom_call_target="Cholesky" | custom-call | tf_op jit(solution)/shard_map/jit(cholesky)/cholesky | solution.py:69
  298.9 9.8 %custom-call.20 = f32[1,128,128]{1,2,0:T(8,128)S(1)} custom-call(f32[1,128,128]{2,1,0:T(8,128)S(1)} %get-tuple-element.148), custom_call_target="InvertDiagBlocksLowerTriangular" | custom-call | tf_op jit(solution)/shard_map/jit(cholesky)/cholesky | solution.py:69
  309.2 11.7 %cholesky.189 = f32[128,128]{1,0:T(8,128)S(1)} custom-call(f32[128,128]{1,0:T(8,128)S(1)} %convolution_subtract_fusion.3), custom_call_target="Cholesky" | custom-call | tf_op jit(solution)/shard_map/jit(cholesky)/cholesky | solution.py:69
  323.5 4.3 while.16
  327.8 19.8 %custom-call.15 = f32[2,128,128]{1,2,0:T(8,128)S(1)} custom-call(f32[2,128,128]{2,1,0:T(8,128)S(1)} %get-tuple-element.47), custom_call_target="InvertDiagBlocksLowerTriangular" | custom-call | tf_op jit(solution)/shard_map/jit(_solve_triangular)/triangular_solve | solution.py:72
  349.1 1.9 collective-permute-start
  355.2 11.7 %cholesky.206 = f32[128,128]{1,0:T(8,128)S(1)} custom-call(f32[128,128]{1,0:T(8,128)S(1)} %cholesky.273), custom_call_target="Cholesky" | custom-call | tf_op jit(solution)/shard_map/jit(cholesky)/cholesky | solution.py:69
  366.9 9.8 %custom-call.21 = f32[1,128,128]{1,2,0:T(8,128)S(1)} custom-call(f32[1,128,128]{2,1,0:T(8,128)S(1)} %get-tuple-element.146), custom_call_target="InvertDiagBlocksLowerTriangular" | custom-call | tf_op jit(solution)/shard_map/jit(cholesky)/cholesky | solution.py:69
  377.2 11.7 %cholesky.223 = f32[128,128]{1,0:T(8,128)S(1)} custom-call(f32[128,128]{1,0:T(8,128)S(1)} %convolution_subtract_fusion.2), custom_call_target="Cholesky" | custom-call | tf_op jit(solution)/shard_map/jit(cholesky)/cholesky | solution.py:69
  391.6 4.3 while.18
  395.9 19.7 %custom-call.22 = f32[2,128,128]{1,2,0:T(8,128)S(1)} custom-call(f32[2,128,128]{2,1,0:T(8,128)S(1)} %get-tuple-element.72), custom_call_target="InvertDiagBlocksLowerTriangular" | custom-call | tf_op jit(solution)/shard_map/jit(_solve_triangular)/triangular_solve | solution.py:72
  417.7 2.2 collective-permute-start.1
  421.1 6.3 %collective-permute-done.1 = f32[256,256]{0,1:T(8,128)S(1)} collective-permute-done((f32[256,256]{0,1:T(8,128)S(1)}, f32[256,256]{0,1:T(8,128)S(1)}, u32[]{:S(2)}, u32[]{:S(2)}) %collective-permute-start.1) | collective-permute-done | bytes 262176 | tf_op jit(solution)/shard_map/ppermute | solution.py:23
  430.0 11.7 %cholesky.240 = f32[128,128]{1,0:T(8,128)S(1)} custom-call(f32[128,128]{1,0:T(8,128)S(1)} %cholesky.276), custom_call_target="Cholesky" | custom-call | tf_op jit(solution)/shard_map/jit(cholesky)/cholesky | solution.py:69
  441.8 9.8 %custom-call.23 = f32[1,128,128]{1,2,0:T(8,128)S(1)} custom-call(f32[1,128,128]{2,1,0:T(8,128)S(1)} %get-tuple-element.142), custom_call_target="InvertDiagBlocksLowerTriangular" | custom-call | tf_op jit(solution)/shard_map/jit(cholesky)/cholesky | solution.py:69
  452.1 11.7 %cholesky.257 = f32[128,128]{1,0:T(8,128)S(1)} custom-call(f32[128,128]{1,0:T(8,128)S(1)} %convolution_subtract_fusion.1), custom_call_target="Cholesky" | custom-call | tf_op jit(solution)/shard_map/jit(cholesky)/cholesky | solution.py:69
  466.5 4.3 while.19
  470.8 19.7 %custom-call.24 = f32[2,128,128]{1,2,0:T(8,128)S(1)} custom-call(f32[2,128,128]{2,1,0:T(8,128)S(1)} %get-tuple-element.73), custom_call_target="InvertDiagBlocksLowerTriangular" | custom-call | tf_op jit(solution)/shard_map/jit(_solve_triangular)/triangular_solve | solution.py:72
  492.0 1.7 convolution_bitcast_fusion.2
  (282 shorter events, 128.3 us)
Async XLA Ops:
  0.6 170.7 %copy-start = (f32[3,1024]{1,0:T(4,128)S(1)}, f32[3,1024]{1,0:T(4,128)}, u32[]{:S(2)}) copy-start(f32[3,1024]{1,0:T(4,128)} %param.10) | copy-start | bytes 36868
  29.2 18.5 %copy-start.1 = (bf16[3,128]{1,0:T(4,128)(2,1)S(1)}, bf16[3,128]{1,0:T(4,128)(2,1)}, u32[]{:S(2)}) copy-start(bf16[3,128]{1,0:T(4,128)(2,1)} %param.11) | copy-start | bytes 2308
  29.2 142.2 %all-to-all-start = ((bf16[64,256,128]{1,2,0:T(8,128)(2,1)}), bf16[64,256,128]{1,2,0:T(8,128)(2,1)}, u32[]{:S(2)}, u32[]{:S(2)}) async-start(bf16[64,256,128]{1,2,0:T(8,128)(2,1)} %stack.8), calls=%async_computation | async-start | bytes 8388608 | tf_op jit(solution)/shard_map/all_to_all | solution.py:10
  349.1 3.4 collective-permute-start
  417.7 9.7 %collective-permute-start.1 = (f32[256,256]{0,1:T(8,128)S(1)}, f32[256,256]{0,1:T(8,128)S(1)}, u32[]{:S(2)}, u32[]{:S(2)}) collective-permute-start(f32[256,256]{0,1:T(8,128)S(1)} %fusion.30), channel_id=1, source_target_pairs={{0,16},{8,24},{16,0},{24,8},{32,48},{40,56},{48,32},{56,40},{64,80... | collective-permute-start | bytes 786440 | tf_op jit(solution)/shard_map/ppermute | solution.py:23
